TPU v7x, 32 devices: a whole 2x2x4 slice. The times are simulated.
32 devices in a mesh: gx: 4 (over y, core), gy: 8 (over z, x).
Axes of the slice: x: 2, y: 2, z: 4, core: 2. Of those that a mesh axis runs over, the one named last changes fastest.
Arguments:
- right_side: float32 [256, 256, 512], P('gx', 'gy'), may hold values from -120 to 120
- diagonal: float32 [256, 256, 512], P('gx', 'gy'), may hold values from 0.002 to 0.2
Outputs:
- update: float32 [256, 256, 512], P('gx', 'gy')
- residual: float32 [256, 256, 512], P('gx', 'gy')
All inputs are finite; a program needn't handle non-finite values.
Results may differ from a plain program's by a relative error of at most 0.00028.
Values sent between devices are 32-bit elements; how exact they have to be, the bound alone decides.
A program may use at most 128 MiB of HBM per device.

v0:
```python
import functools

import jax
import jax.numpy as jnp
from jax import lax
from jax.experimental import pallas as pl
from jax.experimental.pallas import tpu as pltpu
from jax.sharding import PartitionSpec as P

relax_weight = 0.8
coarse_sweeps = 8
MESH = pl.DeviceIdType.MESH
f32 = jnp.float32


def iota(shape, dim):
    return lax.broadcasted_iota(jnp.int32, shape, dim)


def inverse_of(value):
    guess = pl.reciprocal(value, approx=True)
    return guess * (2.0 * relax_weight - relax_weight * value * guess)


def split_dot(value, table):
    rows = value.shape[0]
    high = value.astype(jnp.bfloat16)
    low = (value - high.astype(f32)).astype(jnp.bfloat16)
    both = jnp.dot(jnp.concatenate([high, low], axis=0), table, preferred_element_type=f32)
    return both[:rows] + both[rows:]


def plane_neighbours(plane, below, above):
    rows, lanes = plane.shape
    sub, lane = iota((8, 128), 0), iota((8, 128), 1)
    n_rows, n_lanes = rows // 8, lanes // 128
    tiles = [
        [plane[r * 8:r * 8 + 8, b * 128:b * 128 + 128] for b in range(n_lanes)]
        for r in range(n_rows)]
    lower = [[pltpu.roll(tile, 1, 0) for tile in line] for line in tiles]
    upper = [[pltpu.roll(tile, 7, 0) for tile in line] for line in tiles]
    total = []
    for r in range(n_rows):
        left = [pltpu.roll(tile, 1, 1) for tile in tiles[r]]
        right = [pltpu.roll(tile, 127, 1) for tile in tiles[r]]
        line = []
        for b in range(n_lanes):
            edge = slice(b * 128, b * 128 + 128)
            low = lower[r - 1][b] if r else below[:, edge]
            high = upper[r + 1][b] if r < n_rows - 1 else above[:, edge]
            far_left = left[b - 1] if b else 0.0
            far_right = right[b + 1] if b < n_lanes - 1 else 0.0
            line.append(
                (jnp.where(sub == 0, low, lower[r][b]) + jnp.where(sub == 7, high, upper[r][b]))
                + (jnp.where(lane == 0, far_left, left[b])
                   + jnp.where(lane == 127, far_right, right[b])))
        total.append(jnp.concatenate(line, axis=1) if n_lanes > 1 else line[0])
    return jnp.concatenate(total, axis=0) if n_rows > 1 else total[0]


def kernel(
    n_gx, n_gy, nx, ny, nz,
    rs_hbm, dg_hbm, p0, im0, rs, alpha_ref,
    dg, inv0, g0, q0, ysrc0, ydst0, ysrcq, ydstq,
    pair1, inv1, g1, ysrc1, ydst1, dup1,
    pair2, inv2, g2, ysrc2, ydst2, dup2,
    pair3, gathered, sol, bands, expanded, sums,
    down0, down1, up0, up1, up3,
    load_sem, face_send, face_recv,
    piece_send, piece_recv, line_send, line_recv, twin_send, twin_recv, sum_send, sum_recv,
):
    ax, ay = lax.axis_index("gx"), lax.axis_index("gy")
    chunk = 8
    n_chunks = nx // chunk
    nx1, ny1, nz1 = nx // 2, ny // 2, nz // 2
    nx2, ny2, nz2 = nx // 4, ny // 4, nz // 4
    nx3, ny3, nz3 = nx // 8, ny // 8, nz // 8
    n_all = n_gx * n_gy
    n_same = n_all // 2
    core, me = ax % 2, ax * n_gy + ay
    place = ax // 2 * n_gy + ay

    def load(part, c):
        source, target = ((rs_hbm, rs), (dg_hbm, dg))[part]
        span = pl.ds(c * chunk, chunk)
        return pltpu.make_async_copy(source.at[span], target.at[span], load_sem.at[part, c])

    for c in range(n_chunks):
        load(0, c).start()
        load(1, c).start()

    barrier = pltpu.get_barrier_semaphore()

    def other(k):
        device = lax.rem(me + k, n_all)
        return (device // n_gy, device % n_gy)

    def greet(k, carry):
        pl.semaphore_signal(barrier, inc=1, device_id=other(k), device_id_type=MESH)
        return carry

    lax.fori_loop(1, n_all, greet, 0)

    def down_table(ref):
        row, column = iota(ref.shape, 0), iota(ref.shape, 1)
        ref[...] = jnp.where((row >> 1) == column, 0.125, 0.0).astype(jnp.bfloat16)

    def up_table(ref, shift):
        row, column = iota(ref.shape, 0), iota(ref.shape, 1)
        ref[...] = jnp.where(row == (column >> shift), 1.0, 0.0).astype(jnp.bfloat16)

    down_table(down0)
    down_table(down1)
    up_table(up0, 1)
    up_table(up1, 1)
    up_table(up3, 3)
    sol[...] = jnp.zeros(sol.shape, f32)

    sides = (
        (ax > 0, (ax - 1, ay)),
        (ax < n_gx - 1, (ax + 1, ay)),
        (ay > 0, (ax, ay - 1)),
        (ay < n_gy - 1, (ax, ay + 1)),
    )

    def faces(group, field, ysrc, ydst, n_sides=4):
        count = ysrc.shape[1]
        pairs = (
            (field.at[1], field.at[count + 1]),
            (field.at[count], field.at[0]),
            (ysrc.at[0], ydst.at[1]),
            (ysrc.at[1], ydst.at[0]),
        )
        copies = []
        for side, (source, target) in enumerate(pairs[:n_sides]):
            there, device = sides[side]
            copies.append((there, pltpu.make_async_remote_copy(
                src_ref=source, dst_ref=target,
                send_sem=face_send.at[group, side], recv_sem=face_recv.at[group, side ^ 1],
                device_id=device, device_id_type=MESH,
            )))
        return copies

    def start_faces(copies):
        for there, copy in copies:
            pl.when(there)(copy.start)

    def clear_faces(field, ydst):
        targets = (field.at[0], field.at[field.shape[0] - 1], ydst.at[0], ydst.at[1])
        for (there, _), target in zip(sides, targets):
            @pl.when(jnp.logical_not(there))
            def _():
                target[...] = jnp.zeros(target.shape, f32)

    def wait_faces(group, field, ysrc, ydst, n_sides=4):
        count = ysrc.shape[1]
        targets = (field.at[0], field.at[count + 1], ydst.at[0], ydst.at[1])
        for side, target in enumerate(targets[:n_sides]):
            there, device = sides[side]
            copy = pltpu.make_async_remote_copy(
                src_ref=target, dst_ref=target,
                send_sem=face_send.at[group, side], recv_sem=face_recv.at[group, side],
                device_id=device, device_id_type=MESH,
            )
            pl.when(there)(copy.wait_recv)

    def piece(group, ysrc, ydst, c, side):
        span = pl.ds(c * chunk, chunk)
        there, device = sides[2 + side]
        return there, pltpu.make_async_remote_copy(
            src_ref=ysrc.at[side, span], dst_ref=ydst.at[1 - side, span],
            send_sem=piece_send.at[group, side, c], recv_sem=piece_recv.at[group, 1 - side, c],
            device_id=device, device_id_type=MESH,
        )

    def start_piece(group, ysrc, ydst, c):
        for side in range(2):
            there, copy = piece(group, ysrc, ydst, c, side)
            pl.when(there)(copy.start)

    def await_piece(group, ysrc, ydst, c):
        for side in range(2):
            span = pl.ds(c * chunk, chunk)
            there, device = sides[2 + side]
            copy = pltpu.make_async_remote_copy(
                src_ref=ysrc.at[side, span], dst_ref=ydst.at[side, span],
                send_sem=piece_send.at[group, side, c], recv_sem=piece_recv.at[group, side, c],
                device_id=device, device_id_type=MESH,
            )
            pl.when(there)(copy.wait_recv)

    for field, ydst in ((g0, ydst0), (g1, ydst1), (g2, ydst2), (q0, ydstq)):
        clear_faces(field, ydst)

    def first_chunk(c):
        load(0, c).wait()
        load(1, c).wait()

        stacked = []
        for k in range(chunk // 2):
            j = c * (chunk // 2) + k
            for i in (2 * j, 2 * j + 1):
                inverse = inverse_of(6.0 + dg[i])
                guess = inverse * rs[i]
                inv0[i] = inverse
                g0[i + 1] = guess
                ysrc0[0, i] = guess[:1]
                ysrc0[1, i] = guess[ny - 1:]
            stacked += [rs[2 * j] + rs[2 * j + 1], dg[2 * j] + dg[2 * j + 1]]
        thin = split_dot(jnp.concatenate(stacked, axis=0), down0[...])
        for k in range(chunk // 2):
            for part in range(2):
                first = (2 * k + part) * ny
                for b in range(nz1 // 128):
                    pair1[part, b, c * (chunk // 2) + k] = thin[first:first + ny, b * 128:(b + 1) * 128]

    def first_step(c, carry):
        first_chunk(c)
        start_piece(0, ysrc0, ydst0, c)
        return carry

    first_chunk(0)
    pl.semaphore_wait(barrier, n_all - 1)
    start_piece(0, ysrc0, ydst0, 0)
    lax.fori_loop(1, n_chunks, first_step, 0)
    copies0 = faces(0, g0, ysrc0, ydst0, 2)
    start_faces(copies0)

    group = min(16, nx1)

    def mid_group(h, carry):
        def halved(part, i):
            return jnp.concatenate([
                pair1[part, b, i, pl.ds(0, ny1, 2), :] + pair1[part, b, i, pl.ds(1, ny1, 2), :]
                for b in range(nz1 // 128)
            ], axis=1)

        stacked = []
        for k in range(group // 2):
            planes = []
            for i in (h * group + 2 * k, h * group + 2 * k + 1):
                res, coef = halved(0, i), halved(1, i)
                inverse = inverse_of(1.5 + coef)
                guess = inverse * res
                inv1[i] = inverse * 0.25
                g1[i + 1] = guess
                ysrc1[0, i] = guess[:1]
                ysrc1[1, i] = guess[ny1 - 1:]
                planes.append((res, coef))
            stacked += [planes[0][0] + planes[1][0], planes[0][1] + planes[1][1]]
        thin = split_dot(jnp.concatenate(stacked, axis=0), down1[...])
        for k in range(group // 2):
            for part in range(2):
                first = (2 * k + part) * ny1
                pair2[part, h * (group // 2) + k] = thin[first:first + ny1]
        return carry

    lax.fori_loop(0, nx1 // group, mid_group, 0)
    copies1 = faces(1, g1, ysrc1, ydst1)
    start_faces(copies1)

    low = []
    for i in range(nx2):
        res, coef = (
            pair2[part, i, pl.ds(0, ny2, 2), :] + pair2[part, i, pl.ds(1, ny2, 2), :]
            for part in range(2))
        inverse = inverse_of(0.375 + coef)
        guess = inverse * res
        inv2[i] = inverse * 0.0625
        g2[i + 1] = guess
        ysrc2[0, i] = guess[:1]
        ysrc2[1, i] = guess[ny2 - 1:]
        low.append((res, coef))
    stacked = [
        jnp.concatenate([low[2 * k][part] + low[2 * k + 1][part] for part in range(2)], axis=1)
        for k in range(nx3)]
    pair3[...] = split_dot(jnp.concatenate(stacked, axis=0), down1[...])
    for y in range(ny3):
        gathered[core, place, y] = (
            pair3[pl.ds(2 * y, nx3, ny2), :] + pair3[pl.ds(2 * y + 1, nx3, ny2), :])

    def line_copy(k, slot):
        target = lax.rem(place + k, n_same)
        return pltpu.make_async_remote_copy(
            src_ref=gathered.at[core, slot], dst_ref=gathered.at[core, slot],
            send_sem=line_send.at[k], recv_sem=line_recv.at[slot],
            device_id=(target // n_gy * 2 + core, target % n_gy), device_id_type=MESH,
        )

    def line_start(k, carry):
        line_copy(k, place).start()
        return carry

    def line_wait(k, carry):
        line_copy(k, lax.rem(place + k, n_same)).wait_recv()
        return carry

    def twin_copy(slot):
        return pltpu.make_async_remote_copy(
            src_ref=gathered.at[slot], dst_ref=gathered.at[slot],
            send_sem=twin_send.at[0], recv_sem=twin_recv.at[0],
            device_id=(ax + 1 - 2 * core, ay), device_id_type=MESH,
        )

    lax.fori_loop(1, n_same, line_start, 0)
    copies2 = faces(2, g2, ysrc2, ydst2)
    start_faces(copies2)

    wait_faces(0, g0, ysrc0, ydst0, 2)

    def fine_smooth(c, carry):
        await_piece(0, ysrc0, ydst0, c)
        for k in range(chunk):
            i = c * chunk + k
            plane = g0[i + 1]
            total = g0[i] + g0[i + 2] + plane_neighbours(plane, ydst0[0, i], ydst0[1, i])
            q0[i + 1] = (2.0 - relax_weight) * plane + inv0[i] * total
        return carry

    lax.fori_loop(0, n_chunks, fine_smooth, 0)

    wait_faces(2, g2, ysrc2, ydst2)
    for i in range(nx2):
        plane = g2[i + 1]
        total = g2[i] + g2[i + 2] + plane_neighbours(plane, ydst2[0, i], ydst2[1, i])
        smooth = (2.0 - relax_weight) * plane + inv2[i] * total
        dup2[i, pl.ds(0, ny2, 2), :] = smooth
        dup2[i, pl.ds(1, ny2, 2), :] = smooth

    wait_faces(1, g1, ysrc1, ydst1)

    def mid_smooth(h, carry):
        source = dup2[pl.ds(h * (group // 2), group // 2)]
        wide = split_dot(source.reshape(group // 2 * ny1, nz2), up1[...])
        for k in range(group):
            i = h * group + k
            plane = g1[i + 1]
            total = g1[i] + g1[i + 2] + plane_neighbours(plane, ydst1[0, i], ydst1[1, i])
            smooth = (2.0 - relax_weight) * plane + inv1[i] * total
            smooth += wide[k // 2 * ny1:(k // 2 + 1) * ny1]
            for b in range(nz1 // 128):
                part = smooth[:, b * 128:(b + 1) * 128]
                dup1[b, i, pl.ds(0, ny1, 2), :] = part
                dup1[b, i, pl.ds(1, ny1, 2), :] = part
        return carry

    lax.fori_loop(0, nx1 // group, mid_smooth, 0)

    lax.fori_loop(1, n_same, line_wait, 0)
    twin_copy(core).start()

    step_chunks = 2 if n_chunks % 2 == 0 else 1
    step = step_chunks * chunk

    def carry_up(c, carry):
        span = pl.ds(c * (step // 2), step // 2)
        source = jnp.concatenate(
            [dup1[b, span].reshape(step // 2 * ny, 128) for b in range(nz1 // 128)], axis=1)
        wide = split_dot(source, up0[...])
        for k in range(step):
            i = c * step + k
            smooth = q0[i + 1] + wide[k // 2 * ny:(k // 2 + 1) * ny]
            q0[i + 1] = smooth
            ysrcq[0, i] = smooth[:1]
            ysrcq[1, i] = smooth[ny - 1:]
        for k in range(step_chunks):
            start_piece(1, ysrcq, ydstq, c * step_chunks + k)
        return carry

    lax.fori_loop(0, n_chunks // step_chunks, carry_up, 0)
    copiesq = faces(3, q0, ysrcq, ydstq, 2)
    start_faces(copiesq)

    twin_copy(1 - core).wait_recv()

    wx3, wy3 = nx3 * n_gx, ny3 * n_gy
    hy3 = wy3 // 2
    lanes = 2 * nz3

    def whole(first):
        return jnp.concatenate([
            gathered[a % 2, a // 2 * n_gy + first:a // 2 * n_gy + first + n_gy // 2]
            .reshape(hy3, nx3, lanes) for a in range(n_gx)
        ], axis=1)

    lower, upper = whole(0), whole(n_gy // 2)
    shape = (hy3, wx3, lanes)
    lane, row, level = iota(shape, 2), iota(shape, 1), iota(shape, 0)
    is_low = lane < nz3
    res3 = jnp.where(is_low, lower, pltpu.roll(upper, nz3, 2))
    coef3 = jnp.where(is_low, pltpu.roll(lower, nz3, 2), upper)
    scale3 = 0.25**3
    inverse3 = relax_weight / (6.0 * scale3 + coef3)
    step3 = inverse3 * scale3
    guess3 = inverse3 * res3
    depth = jnp.where(is_low, lane, lane - nz3)
    no_left, no_right = depth == 0, depth == nz3 - 1
    no_down, no_up = row == 0, row == wx3 - 1
    flat_low = iota((1, wx3, lanes), 2) < nz3

    def coarse_neighbours(field):
        first = jnp.where(flat_low, 0.0, pltpu.roll(field[hy3 - 1:], nz3, 2))
        last = jnp.where(flat_low, pltpu.roll(field[:1], nz3, 2), 0.0)
        total = jnp.concatenate([first, field[:hy3 - 1]], axis=0)
        total += jnp.concatenate([field[1:], last], axis=0)
        total += jnp.where(no_down, 0.0, pltpu.roll(field, 1, 1))
        total += jnp.where(no_up, 0.0, pltpu.roll(field, wx3 - 1, 1))
        total += jnp.where(no_left, 0.0, pltpu.roll(field, 1, 2))
        return total + jnp.where(no_right, 0.0, pltpu.roll(field, lanes - 1, 2))

    jac = guess3
    for _ in range(coarse_sweeps - 1):
        jac = (1.0 - relax_weight) * jac + guess3 + step3 * coarse_neighbours(jac)

    def one(flag):
        return jnp.where(flag, 1.0, 0.0)

    ends = one(no_left) + one(no_right) + one(no_down) + one(no_up)
    ends += one(jnp.logical_and(level == 0, is_low))
    ends += one(jnp.logical_and(level == hy3 - 1, jnp.logical_not(is_low)))
    ones_image = scale3 * ends + coef3
    shift = jnp.sum(res3 - ones_image * jac) / jnp.sum(ones_image)
    jac = jac + shift

    sol[1:hy3 + 1, nx3:nx3 + wx3, :] = jnp.where(is_low, jac, 0.0)
    sol[hy3 + 1:wy3 + 1, nx3:nx3 + wx3, :] = jnp.where(is_low, pltpu.roll(jac, nz3, 2), 0.0)

    near = sol[pl.ds(ay * ny3, ny3 + 2), pl.ds(pl.multiple_of(ax * nx3, nx3), 3 * nx3), :]
    wide = split_dot(near.reshape((ny3 + 2) * 3 * nx3, lanes), up3[...])
    expanded[...] = wide.reshape(ny3 + 2, 3 * nx3, nz)
    for y in range(ny3):
        around = expanded[y + 1]
        own = around[nx3:2 * nx3]
        column = iota(own.shape, 1)
        bands[0, y] = own
        bands[1, y] = (
            2.0 * own
            - jnp.where(column == 0, 0.0, pltpu.roll(own, 1, 1))
            - jnp.where(column == nz - 1, 0.0, pltpu.roll(own, nz - 1, 1)))
        bands[2, y] = own - expanded[y, nx3:2 * nx3]
        bands[3, y] = own - expanded[y + 2, nx3:2 * nx3]
        bands[4, y] = own - pltpu.roll(around, 1, 0)[nx3:2 * nx3]
        bands[5, y] = own - pltpu.roll(around, 3 * nx3 - 1, 0)[nx3:2 * nx3]

    wait_faces(3, q0, ysrcq, ydstq, 2)

    fold = ny // ny3

    def fold_plane(value):
        total = value.reshape(ny // 8, 8, nz).sum(axis=0)
        return sum(total[:, b * 128:(b + 1) * 128] for b in range(nz // 128))

    def last_chunk(c, carry):
        await_piece(1, ysrcq, ydstq, c)

        def rows(kind):
            return [
                jnp.broadcast_to(bands[kind, y, pl.ds(c, 1), :], (fold, nz)) for y in range(ny3)]

        def laid(parts):
            return jnp.concatenate(parts, axis=0)

        sub = iota((fold, nz), 0)
        own = laid(rows(0))
        edge = laid([
            flat + jnp.where(sub == 0, down, 0.0) + jnp.where(sub == fold - 1, up, 0.0)
            for flat, down, up in zip(rows(1), rows(2), rows(3))])
        rz, zq = carry
        for k in range(chunk):
            i = c * chunk + k
            plane = q0[i + 1]
            near_sum = q0[i] + q0[i + 2] + plane_neighbours(plane, ydstq[0, i], ydstq[1, i])
            precond = plane + own
            image = 6.0 * plane - near_sum + dg[i] * precond + edge
            if k == 0:
                image += laid(rows(4))
            if k == chunk - 1:
                image += laid(rows(5))
            p0[i] = precond
            im0[i] = image
            rz += fold_plane(rs[i] * precond)
            zq += fold_plane(precond * image)
        return rz, zq

    zero = jnp.zeros((8, 128), f32)
    rz, zq = lax.fori_loop(0, n_chunks, last_chunk, (zero, zero))

    def sum_copy(k, slot):
        return pltpu.make_async_remote_copy(
            src_ref=sums.at[slot], dst_ref=sums.at[slot],
            send_sem=sum_send.at[k], recv_sem=sum_recv.at[slot],
            device_id=other(k), device_id_type=MESH,
        )

    def sum_start(k, carry):
        sum_copy(k, me).start()
        return carry

    def sum_wait(k, carry):
        sum_copy(k, lax.rem(me + k, n_all)).wait_recv()
        return carry

    sums[me] = jnp.concatenate(
        [rz.sum(axis=0, keepdims=True), zq.sum(axis=0, keepdims=True)], axis=0)
    lax.fori_loop(1, n_all, sum_start, 0)
    lax.fori_loop(1, n_all, sum_wait, 0)
    total = sum(sums[k] for k in range(n_all))
    both = jnp.sum(total, axis=1, keepdims=True)
    alpha_ref[...] = jnp.broadcast_to(both[:1] / both[1:], alpha_ref.shape)

    for copies in (copies0, copies1, copies2, copiesq):
        for there, copy in copies:
            pl.when(there)(copy.wait_send)

    def pieces_sent(c, carry):
        for group, (ysrc, ydst) in enumerate(((ysrc0, ydst0), (ysrcq, ydstq))):
            for side in range(2):
                there, copy = piece(group, ysrc, ydst, c, side)
                pl.when(there)(copy.wait_send)
        return carry

    lax.fori_loop(0, n_chunks, pieces_sent, 0)

    def line_sent(k, carry):
        line_copy(k, place).wait_send()
        return carry

    def sum_sent(k, carry):
        sum_copy(k, me).wait_send()
        return carry

    lax.fori_loop(1, n_same, line_sent, 0)
    twin_copy(core).wait_send()
    lax.fori_loop(1, n_all, sum_sent, 0)


def scale_kernel(nx, precond, image, right, alpha_ref, update_hbm, residual_hbm, update, residual, sem):
    chunk = 8

    def store(part, c):
        source, target = ((update, update_hbm), (residual, residual_hbm))[part]
        span = pl.ds(c * chunk, chunk)
        return pltpu.make_async_copy(source.at[span], target.at[span], sem.at[part, c])

    alpha = alpha_ref[:1, :1]

    def step(c, carry):
        for k in range(chunk):
            update[c * chunk + k] = alpha * precond[c * chunk + k]
        store(0, c).start()
        for k in range(chunk):
            i = c * chunk + k
            residual[i] = right[i] - alpha * image[i]
        store(1, c).start()
        return carry

    lax.fori_loop(0, nx // chunk, step, 0)

    def finish(c, carry):
        store(0, c).wait()
        store(1, c).wait()
        return carry

    lax.fori_loop(0, nx // chunk, finish, 0)


def body(right_side, diagonal):
    n_gx, n_gy = lax.axis_size("gx"), lax.axis_size("gy")
    nx, ny, nz = right_side.shape
    V = lambda *shape: pltpu.VMEM(shape, f32)
    B = lambda *shape: pltpu.VMEM(shape, jnp.bfloat16)
    D = lambda *shape: pltpu.SemaphoreType.DMA(shape)
    nx1, ny1, nz1 = nx // 2, ny // 2, nz // 2
    nx2, ny2, nz2 = nx // 4, ny // 4, nz // 4
    nx3, ny3, nz3 = nx // 8, ny // 8, nz // 8
    block = V(nx, ny, nz)
    scratch = [
        block, block, V(nx + 2, ny, nz), V(nx + 2, ny, nz),
        V(2, nx, 1, nz), V(2, nx, 1, nz), V(2, nx, 1, nz), V(2, nx, 1, nz),
        V(2, nz1 // 128, nx1, ny, 128), V(nx1, ny1, nz1), V(nx1 + 2, ny1, nz1),
        V(2, nx1, 1, nz1), V(2, nx1, 1, nz1), V(nz1 // 128, nx1, ny, 128),
        V(2, nx2, ny1, nz2), V(nx2, ny2, nz2), V(nx2 + 2, ny2, nz2),
        V(2, nx2, 1, nz2), V(2, nx2, 1, nz2), V(nx2, ny1, nz2),
        V(nx3 * ny2, 2 * nz3), V(2, n_gx // 2 * n_gy, ny3, nx3, 2 * nz3),
        V(ny3 * n_gy + 2, nx3 * (n_gx + 2), 2 * nz3), V(6, ny3, nx3, nz), V(ny3 + 2, 3 * nx3, nz),
        V(n_gx * n_gy, 2, 128),
        B(nz, nz1), B(nz1, nz2),
        B(nz1, nz), B(nz2, nz1), B(2 * nz3, nz),
        D(2, nx // 8), D(4, 4), D(4, 4), D(2, 2, nx // 8), D(2, 2, nx // 8),
        D(n_gx * n_gy), D(n_gx * n_gy), D(1), D(1), D(n_gx * n_gy), D(n_gx * n_gy),
    ]
    precond, image, right, alpha = pl.pallas_call(
        functools.partial(kernel, n_gx, n_gy, nx, ny, nz),
        out_shape=(block, block, block, V(8, 128)),
        in_specs=[pl.BlockSpec(memory_space=pl.ANY)] * 2,
        out_specs=[pl.BlockSpec(memory_space=pltpu.VMEM)] * 4,
        scratch_shapes=scratch,
        compiler_params=pltpu.CompilerParams(
            collective_id=0, has_side_effects=True, vmem_limit_bytes=40 * 1024 * 1024),
        name="cycle",
    )(right_side, diagonal)
    whole = jax.ShapeDtypeStruct(right_side.shape, f32)
    return pl.pallas_call(
        functools.partial(scale_kernel, nx),
        out_shape=(whole, whole),
        in_specs=[pl.BlockSpec(memory_space=pltpu.VMEM)] * 4,
        out_specs=[pl.BlockSpec(memory_space=pl.ANY)] * 2,
        scratch_shapes=[block, block, D(2, nx // 8)],
        compiler_params=pltpu.CompilerParams(vmem_limit_bytes=24 * 1024 * 1024),
        name="scale",
    )(precond, image, right, alpha)


def solution(mesh):
    placed = (P("gx", "gy", None), P("gx", "gy", None))
    return jax.shard_map(
        body,
        mesh=mesh,
        in_specs=placed,
        out_specs=(P("gx", "gy", None), P("gx", "gy", None)),
        check_vma=False,
    )
```

profile of v0, /device:TPU:0, one launch (start us, length us, event | category | flops | bytes accessed | tf_op | source)
XLA Modules:
  0.0 39.9 jit_solution(16306916125216348871)
XLA Ops:
  0.6 35.8 %cycle.1 = (f32[64,32,512]{2,1,0:T(8,128)S(1)}, f32[64,32,512]{2,1,0:T(8,128)S(1)}, f32[64,32,512]{2,1,0:T(8,128)S(1)}, f32[8,128]{1,0:T(8,128)S(1)}) custom-call(f32[64,32,512]{2,1,0:T(8,128)} %rs_hbm.1, f32[64,32,512]{2,1,0:T(8,128)} %dg_hbm.1), custom_call_target="tpu_custom_call" | custom-call | tf_op jit(solution)/shard_map/cycle/pallas_call | solution.py:592
  36.4 3.5 %scale.1 = (f32[64,32,512]{2,1,0:T(8,128)}, f32[64,32,512]{2,1,0:T(8,128)}) custom-call(f32[64,32,512]{2,1,0:T(8,128)S(1)} %get-tuple-element.6.precond, f32[64,32,512]{2,1,0:T(8,128)S(1)} %get-tuple-element.7.image, f32[64,32,512]{2,1,0:T(8,128)S(1)} %get-tuple-element.8.right, f32[8,128]{1,0:T(8,128)S(1)} %get-tuple-element.9.alpha_ref), custom_call_target="tpu_custom_call" | custom-call | tf_op jit(solution)/shard_map/scale/pallas_call | solution.py:603
where the time goes:
time: 40.1 us; the launch traced here: 39.9 us
  Pallas kernels  39.3 us (98%)
  between operations  0.64 us (2%)
    pallas_call x1, Pallas kernels, body(): pl.pallas_call(functools.partial(kernel, n_gx, n_gy, nx, ny, nz), out_sha...  35.8 us
    pallas_call x1, Pallas kernels, body(): pl.pallas_call(functools.partial(scale_kernel, nx), out_shape=(whole, who...  3.48 us

commit v1 on v0

--- a/solution.py
+++ b/solution.py
@@ -22,40 +22,59 @@
     return guess * (2.0 * relax_weight - relax_weight * value * guess)
 
 
+def split(value):
+    high = value.astype(jnp.bfloat16)
+    return high, (value - high.astype(f32)).astype(jnp.bfloat16)
+
+
+def joined_dot(parts, table):
+    rows = sum(high.shape[0] for high, _ in parts)
+    stacked = [high for high, _ in parts] + [low for _, low in parts]
+    both = jnp.dot(jnp.concatenate(stacked, axis=0), table, preferred_element_type=f32)
+    return both[:rows] + both[rows:]
+
+
 def split_dot(value, table):
-    rows = value.shape[0]
-    high = value.astype(jnp.bfloat16)
-    low = (value - high.astype(f32)).astype(jnp.bfloat16)
-    both = jnp.dot(jnp.concatenate([high, low], axis=0), table, preferred_element_type=f32)
-    return both[:rows] + both[rows:]
-
-
-def plane_neighbours(plane, below, above):
+    return joined_dot([split(value)], table)
+
+
+def band(r):
+    return slice(r * 8, r * 8 + 8)
+
+
+def band_neighbours(plane, r, below, above, seam=0):
     rows, lanes = plane.shape
     sub, lane = iota((8, 128), 0), iota((8, 128), 1)
-    n_rows, n_lanes = rows // 8, lanes // 128
-    tiles = [
-        [plane[r * 8:r * 8 + 8, b * 128:b * 128 + 128] for b in range(n_lanes)]
-        for r in range(n_rows)]
-    lower = [[pltpu.roll(tile, 1, 0) for tile in line] for line in tiles]
-    upper = [[pltpu.roll(tile, 7, 0) for tile in line] for line in tiles]
-    total = []
-    for r in range(n_rows):
-        left = [pltpu.roll(tile, 1, 1) for tile in tiles[r]]
-        right = [pltpu.roll(tile, 127, 1) for tile in tiles[r]]
-        line = []
-        for b in range(n_lanes):
-            edge = slice(b * 128, b * 128 + 128)
-            low = lower[r - 1][b] if r else below[:, edge]
-            high = upper[r + 1][b] if r < n_rows - 1 else above[:, edge]
-            far_left = left[b - 1] if b else 0.0
-            far_right = right[b + 1] if b < n_lanes - 1 else 0.0
-            line.append(
-                (jnp.where(sub == 0, low, lower[r][b]) + jnp.where(sub == 7, high, upper[r][b]))
-                + (jnp.where(lane == 0, far_left, left[b])
-                   + jnp.where(lane == 127, far_right, right[b])))
-        total.append(jnp.concatenate(line, axis=1) if n_lanes > 1 else line[0])
-    return jnp.concatenate(total, axis=0) if n_rows > 1 else total[0]
+    first, last = lane == 0, lane == 127
+    if seam:
+        first = jnp.logical_or(first, lane == seam)
+        last = jnp.logical_or(last, lane == seam - 1)
+    centre = plane[band(r), :]
+    low = plane[band(r - 1), :] if r else below
+    high = plane[band(r + 1), :] if r < rows // 8 - 1 else above
+    n_lanes = lanes // 128
+    tiles = [centre[:, b * 128:b * 128 + 128] for b in range(n_lanes)]
+    line = []
+    for b, tile in enumerate(tiles):
+        edge = slice(b * 128, b * 128 + 128)
+        left = tiles[b - 1] if b else 0.0
+        right = tiles[b + 1] if b < n_lanes - 1 else 0.0
+        if seam:
+            across = jnp.where(first, 0.0, pltpu.roll(tile, 1, 1))
+            across += jnp.where(last, 0.0, pltpu.roll(tile, 127, 1))
+        else:
+            across = pltpu.roll(jnp.where(last, left, tile), 1, 1)
+            across += pltpu.roll(jnp.where(first, right, tile), 127, 1)
+        along = pltpu.roll(jnp.where(sub == 7, 0.0 if low is None else low[:, edge], tile), 1, 0)
+        along += pltpu.roll(jnp.where(sub == 0, 0.0 if high is None else high[:, edge], tile), 7, 0)
+        line.append(across + along)
+    return centre, jnp.concatenate(line, axis=1) if n_lanes > 1 else line[0]
+
+
+def smooth_band(field, inverse, ydst, i, r):
+    centre, total = band_neighbours(field.at[i + 1], r, ydst[0, i], ydst[1, i])
+    total += field[i, band(r), :] + field[i + 2, band(r), :]
+    return (2.0 - relax_weight) * centre + inverse[i, band(r), :] * total
 
 
 def kernel(
@@ -64,7 +83,7 @@
     dg, inv0, g0, q0, ysrc0, ydst0, ysrcq, ydstq,
     pair1, inv1, g1, ysrc1, ydst1, dup1,
     pair2, inv2, g2, ysrc2, ydst2, dup2,
-    pair3, gathered, sol, bands, expanded, sums,
+    pair3, gathered, sol, bands, expanded, sums, step_ref, guess_ref, ones_ref, jac_ref,
     down0, down1, up0, up1, up3,
     load_sem, face_send, face_recv,
     piece_send, piece_recv, line_send, line_recv, twin_send, twin_recv, sum_send, sum_recv,
@@ -196,21 +215,29 @@
         load(0, c).wait()
         load(1, c).wait()
 
-        stacked = []
+        res_parts, coef_parts = [], []
         for k in range(chunk // 2):
-            j = c * (chunk // 2) + k
-            for i in (2 * j, 2 * j + 1):
-                inverse = inverse_of(6.0 + dg[i])
-                guess = inverse * rs[i]
-                inv0[i] = inverse
-                g0[i + 1] = guess
-                ysrc0[0, i] = guess[:1]
-                ysrc0[1, i] = guess[ny - 1:]
-            stacked += [rs[2 * j] + rs[2 * j + 1], dg[2 * j] + dg[2 * j + 1]]
-        thin = split_dot(jnp.concatenate(stacked, axis=0), down0[...])
+            pair = (c * chunk + 2 * k, c * chunk + 2 * k + 1)
+            for h in range(ny // 16):
+                rows = slice(h * 16, h * 16 + 16)
+                res_sum = coef_sum = 0.0
+                for i in pair:
+                    res, coef = rs[i, rows, :], dg[i, rows, :]
+                    inverse = inverse_of(6.0 + coef)
+                    guess = inverse * res
+                    inv0[i, rows, :] = inverse
+                    g0[i + 1, rows, :] = guess
+                    if h == 0:
+                        ysrc0[0, i] = guess[:1]
+                    if h == ny // 16 - 1:
+                        ysrc0[1, i] = guess[15:]
+                    res_sum, coef_sum = res_sum + res, coef_sum + coef
+                res_parts.append(split(res_sum))
+                coef_parts.append(split(coef_sum))
+        thin = joined_dot(res_parts + coef_parts, down0[...])
         for k in range(chunk // 2):
             for part in range(2):
-                first = (2 * k + part) * ny
+                first = (part * (chunk // 2) + k) * ny
                 for b in range(nz1 // 128):
                     pair1[part, b, c * (chunk // 2) + k] = thin[first:first + ny, b * 128:(b + 1) * 128]
 
@@ -312,18 +339,15 @@
         await_piece(0, ysrc0, ydst0, c)
         for k in range(chunk):
             i = c * chunk + k
-            plane = g0[i + 1]
-            total = g0[i] + g0[i + 2] + plane_neighbours(plane, ydst0[0, i], ydst0[1, i])
-            q0[i + 1] = (2.0 - relax_weight) * plane + inv0[i] * total
+            for r in range(ny // 8):
+                q0[i + 1, band(r), :] = smooth_band(g0, inv0, ydst0, i, r)
         return carry
 
     lax.fori_loop(0, n_chunks, fine_smooth, 0)
 
     wait_faces(2, g2, ysrc2, ydst2)
     for i in range(nx2):
-        plane = g2[i + 1]
-        total = g2[i] + g2[i + 2] + plane_neighbours(plane, ydst2[0, i], ydst2[1, i])
-        smooth = (2.0 - relax_weight) * plane + inv2[i] * total
+        smooth = jnp.concatenate([smooth_band(g2, inv2, ydst2, i, r) for r in range(ny2 // 8)], axis=0)
         dup2[i, pl.ds(0, ny2, 2), :] = smooth
         dup2[i, pl.ds(1, ny2, 2), :] = smooth
 
@@ -334,9 +358,8 @@
         wide = split_dot(source.reshape(group // 2 * ny1, nz2), up1[...])
         for k in range(group):
             i = h * group + k
-            plane = g1[i + 1]
-            total = g1[i] + g1[i + 2] + plane_neighbours(plane, ydst1[0, i], ydst1[1, i])
-            smooth = (2.0 - relax_weight) * plane + inv1[i] * total
+            smooth = jnp.concatenate(
+                [smooth_band(g1, inv1, ydst1, i, r) for r in range(ny1 // 8)], axis=0)
             smooth += wide[k // 2 * ny1:(k // 2 + 1) * ny1]
             for b in range(nz1 // 128):
                 part = smooth[:, b * 128:(b + 1) * 128]
@@ -394,32 +417,39 @@
     step3 = inverse3 * scale3
     guess3 = inverse3 * res3
     depth = jnp.where(is_low, lane, lane - nz3)
-    no_left, no_right = depth == 0, depth == nz3 - 1
-    no_down, no_up = row == 0, row == wx3 - 1
-    flat_low = iota((1, wx3, lanes), 2) < nz3
-
-    def coarse_neighbours(field):
-        first = jnp.where(flat_low, 0.0, pltpu.roll(field[hy3 - 1:], nz3, 2))
-        last = jnp.where(flat_low, pltpu.roll(field[:1], nz3, 2), 0.0)
-        total = jnp.concatenate([first, field[:hy3 - 1]], axis=0)
-        total += jnp.concatenate([field[1:], last], axis=0)
-        total += jnp.where(no_down, 0.0, pltpu.roll(field, 1, 1))
-        total += jnp.where(no_up, 0.0, pltpu.roll(field, wx3 - 1, 1))
-        total += jnp.where(no_left, 0.0, pltpu.roll(field, 1, 2))
-        return total + jnp.where(no_right, 0.0, pltpu.roll(field, lanes - 1, 2))
-
-    jac = guess3
-    for _ in range(coarse_sweeps - 1):
-        jac = (1.0 - relax_weight) * jac + guess3 + step3 * coarse_neighbours(jac)
+    step_ref[...] = step3
+    guess_ref[...] = guess3
+    flat_low = iota((8, lanes), 1) < nz3
 
     def one(flag):
         return jnp.where(flag, 1.0, 0.0)
 
-    ends = one(no_left) + one(no_right) + one(no_down) + one(no_up)
+    ends = one(depth == 0) + one(depth == nz3 - 1) + one(row == 0) + one(row == wx3 - 1)
     ends += one(jnp.logical_and(level == 0, is_low))
     ends += one(jnp.logical_and(level == hy3 - 1, jnp.logical_not(is_low)))
     ones_image = scale3 * ends + coef3
-    shift = jnp.sum(res3 - ones_image * jac) / jnp.sum(ones_image)
+    ones_ref[...] = ones_image
+    ones_total, res_total = jnp.sum(ones_image), jnp.sum(res3)
+    old = guess_ref
+    for sweep_index in range(coarse_sweeps - 1):
+        new = jac_ref.at[sweep_index % 2]
+        for y in range(hy3):
+            for r in range(wx3 // 8):
+                centre, total = band_neighbours(old.at[y], r, None, None, nz3)
+                if y:
+                    total += old[y - 1, band(r), :]
+                else:
+                    total += jnp.where(flat_low, 0.0, pltpu.roll(old[hy3 - 1, band(r), :], nz3, 1))
+                if y < hy3 - 1:
+                    total += old[y + 1, band(r), :]
+                else:
+                    total += jnp.where(flat_low, pltpu.roll(old[0, band(r), :], nz3, 1), 0.0)
+                new[y, band(r), :] = (
+                    (1.0 - relax_weight) * centre + guess_ref[y, band(r), :]
+                    + step_ref[y, band(r), :] * total)
+        old = new
+    jac = old[...]
+    shift = (res_total - jnp.sum(ones_ref[...] * jac)) / ones_total
     jac = jac + shift
 
     sol[1:hy3 + 1, nx3:nx3 + wx3, :] = jnp.where(is_low, jac, 0.0)
@@ -446,10 +476,6 @@
 
     fold = ny // ny3
 
-    def fold_plane(value):
-        total = value.reshape(ny // 8, 8, nz).sum(axis=0)
-        return sum(total[:, b * 128:(b + 1) * 128] for b in range(nz // 128))
-
     def last_chunk(c, carry):
         await_piece(1, ysrcq, ydstq, c)
 
@@ -457,33 +483,34 @@
             return [
                 jnp.broadcast_to(bands[kind, y, pl.ds(c, 1), :], (fold, nz)) for y in range(ny3)]
 
-        def laid(parts):
-            return jnp.concatenate(parts, axis=0)
-
         sub = iota((fold, nz), 0)
-        own = laid(rows(0))
-        edge = laid([
-            flat + jnp.where(sub == 0, down, 0.0) + jnp.where(sub == fold - 1, up, 0.0)
-            for flat, down, up in zip(rows(1), rows(2), rows(3))])
         rz, zq = carry
-        for k in range(chunk):
-            i = c * chunk + k
-            plane = q0[i + 1]
-            near_sum = q0[i] + q0[i + 2] + plane_neighbours(plane, ydstq[0, i], ydstq[1, i])
-            precond = plane + own
-            image = 6.0 * plane - near_sum + dg[i] * precond + edge
-            if k == 0:
-                image += laid(rows(4))
-            if k == chunk - 1:
-                image += laid(rows(5))
-            p0[i] = precond
-            im0[i] = image
-            rz += fold_plane(rs[i] * precond)
-            zq += fold_plane(precond * image)
+        kinds = [rows(kind) for kind in range(6)]
+        for r in range(ny // 8):
+            own, flat, down, up, back, ahead = (kind[r] for kind in kinds)
+            edge = flat + jnp.where(sub == 0, down, 0.0) + jnp.where(sub == fold - 1, up, 0.0)
+            for k in range(chunk):
+                i = c * chunk + k
+                centre, near_sum = band_neighbours(q0.at[i + 1], r, ydstq[0, i], ydstq[1, i])
+                near_sum += q0[i, band(r), :] + q0[i + 2, band(r), :]
+                precond = centre + own
+                image = 6.0 * centre - near_sum + dg[i, band(r), :] * precond + edge
+                if k == 0:
+                    image += back
+                if k == chunk - 1:
+                    image += ahead
+                p0[i, band(r), :] = precond
+                im0[i, band(r), :] = image
+                rz += rs[i, band(r), :] * precond
+                zq += precond * image
         return rz, zq
 
-    zero = jnp.zeros((8, 128), f32)
+    zero = jnp.zeros((fold, nz), f32)
     rz, zq = lax.fori_loop(0, n_chunks, last_chunk, (zero, zero))
+
+    def folded(value):
+        line = value.sum(axis=0, keepdims=True)
+        return sum(line[:, b * 128:(b + 1) * 128] for b in range(nz // 128))
 
     def sum_copy(k, slot):
         return pltpu.make_async_remote_copy(
@@ -501,7 +528,7 @@
         return carry
 
     sums[me] = jnp.concatenate(
-        [rz.sum(axis=0, keepdims=True), zq.sum(axis=0, keepdims=True)], axis=0)
+        [folded(rz), folded(zq)], axis=0)
     lax.fori_loop(1, n_all, sum_start, 0)
     lax.fori_loop(1, n_all, sum_wait, 0)
     total = sum(sums[k] for k in range(n_all))
@@ -574,6 +601,7 @@
     nx2, ny2, nz2 = nx // 4, ny // 4, nz // 4
     nx3, ny3, nz3 = nx // 8, ny // 8, nz // 8
     block = V(nx, ny, nz)
+    coarse = V(ny3 * n_gy // 2, nx3 * n_gx, 2 * nz3)
     scratch = [
         block, block, V(nx + 2, ny, nz), V(nx + 2, ny, nz),
         V(2, nx, 1, nz), V(2, nx, 1, nz), V(2, nx, 1, nz), V(2, nx, 1, nz),
@@ -583,7 +611,7 @@
         V(2, nx2, 1, nz2), V(2, nx2, 1, nz2), V(nx2, ny1, nz2),
         V(nx3 * ny2, 2 * nz3), V(2, n_gx // 2 * n_gy, ny3, nx3, 2 * nz3),
         V(ny3 * n_gy + 2, nx3 * (n_gx + 2), 2 * nz3), V(6, ny3, nx3, nz), V(ny3 + 2, 3 * nx3, nz),
-        V(n_gx * n_gy, 2, 128),
+        V(n_gx * n_gy, 2, 128), coarse, coarse, coarse, V(2, *coarse.shape),
         B(nz, nz1), B(nz1, nz2),
         B(nz1, nz), B(nz2, nz1), B(2 * nz3, nz),
         D(2, nx // 8), D(4, 4), D(4, 4), D(2, 2, nx // 8), D(2, 2, nx // 8),

time: 40.1 us -> 39.8 us (level)
  no operation moved by 1% of the time
where the time goes in v1:
time: 39.8 us; the launch traced here: 39.6 us
  Pallas kernels  39 us (98%)
  between operations  0.64 us (2%)
    pallas_call x1, Pallas kernels, body(): pl.pallas_call(functools.partial(kernel, n_gx, n_gy, nx, ny, nz), out_sha...  35.5 us
    pallas_call x1, Pallas kernels, body(): pl.pallas_call(functools.partial(scale_kernel, nx), out_shape=(whole, who...  3.48 us

profile of v1, /device:TPU:0, one launch (start us, length us, event | category | flops | bytes accessed | tf_op | source)
XLA Modules:
  0.0 39.6 jit_solution(16777274312379316887)
XLA Ops:
  0.6 35.5 %cycle.1 = (f32[64,32,512]{2,1,0:T(8,128)S(1)}, f32[64,32,512]{2,1,0:T(8,128)S(1)}, f32[64,32,512]{2,1,0:T(8,128)S(1)}, f32[8,128]{1,0:T(8,128)S(1)}) custom-call(f32[64,32,512]{2,1,0:T(8,128)} %rs_hbm.1, f32[64,32,512]{2,1,0:T(8,128)} %dg_hbm.1), custom_call_target="tpu_custom_call" | custom-call | tf_op jit(solution)/shard_map/cycle/pallas_call | solution.py:620
  36.1 3.5 %scale.1 = (f32[64,32,512]{2,1,0:T(8,128)}, f32[64,32,512]{2,1,0:T(8,128)}) custom-call(f32[64,32,512]{2,1,0:T(8,128)S(1)} %get-tuple-element.6.precond, f32[64,32,512]{2,1,0:T(8,128)S(1)} %get-tuple-element.7.image, f32[64,32,512]{2,1,0:T(8,128)S(1)} %get-tuple-element.8.right, f32[8,128]{1,0:T(8,128)S(1)} %get-tuple-element.9.alpha_ref), custom_call_target="tpu_custom_call" | custom-call | tf_op jit(solution)/shard_map/scale/pallas_call | solution.py:631

commit v2 on v1

--- a/solution.py
+++ b/solution.py
@@ -80,7 +80,7 @@
 def kernel(
     n_gx, n_gy, nx, ny, nz,
     rs_hbm, dg_hbm, p0, im0, rs, alpha_ref,
-    dg, inv0, g0, q0, ysrc0, ydst0, ysrcq, ydstq,
+    dg, inv0, g0, q0, ysrc0, ydst0, ysrcq, ydstq, ysrcw, ydstw, wide_rows,
     pair1, inv1, g1, ysrc1, ydst1, dup1,
     pair2, inv2, g2, ysrc2, ydst2, dup2,
     pair3, gathered, sol, bands, expanded, sums, step_ref, guess_ref, ones_ref, jac_ref,
@@ -208,7 +208,7 @@
             )
             pl.when(there)(copy.wait_recv)
 
-    for field, ydst in ((g0, ydst0), (g1, ydst1), (g2, ydst2), (q0, ydstq)):
+    for field, ydst in ((g0, ydst0), (g1, ydst1), (g2, ydst2), (q0, ydstq), (q0, ydstw)):
         clear_faces(field, ydst)
 
     def first_chunk(c):
@@ -340,7 +340,13 @@
         for k in range(chunk):
             i = c * chunk + k
             for r in range(ny // 8):
-                q0[i + 1, band(r), :] = smooth_band(g0, inv0, ydst0, i, r)
+                smooth = smooth_band(g0, inv0, ydst0, i, r)
+                q0[i + 1, band(r), :] = smooth
+                if r == 0:
+                    ysrcq[0, i] = smooth[:1]
+                if r == ny // 8 - 1:
+                    ysrcq[1, i] = smooth[7:]
+        start_piece(1, ysrcq, ydstq, c)
         return carry
 
     lax.fori_loop(0, n_chunks, fine_smooth, 0)
@@ -361,6 +367,8 @@
             smooth = jnp.concatenate(
                 [smooth_band(g1, inv1, ydst1, i, r) for r in range(ny1 // 8)], axis=0)
             smooth += wide[k // 2 * ny1:(k // 2 + 1) * ny1]
+            ysrcw[0, i] = smooth[:1]
+            ysrcw[1, i] = smooth[ny1 - 1:]
             for b in range(nz1 // 128):
                 part = smooth[:, b * 128:(b + 1) * 128]
                 dup1[b, i, pl.ds(0, ny1, 2), :] = part
@@ -368,6 +376,8 @@
         return carry
 
     lax.fori_loop(0, nx1 // group, mid_smooth, 0)
+    copiesw = faces(3, g1, ysrcw, ydstw)[2:]
+    start_faces(copiesw)
 
     lax.fori_loop(1, n_same, line_wait, 0)
     twin_copy(core).start()
@@ -382,12 +392,7 @@
         wide = split_dot(source, up0[...])
         for k in range(step):
             i = c * step + k
-            smooth = q0[i + 1] + wide[k // 2 * ny:(k // 2 + 1) * ny]
-            q0[i + 1] = smooth
-            ysrcq[0, i] = smooth[:1]
-            ysrcq[1, i] = smooth[ny - 1:]
-        for k in range(step_chunks):
-            start_piece(1, ysrcq, ydstq, c * step_chunks + k)
+            q0[i + 1] = q0[i + 1] + wide[k // 2 * ny:(k // 2 + 1) * ny]
         return carry
 
     lax.fori_loop(0, n_chunks // step_chunks, carry_up, 0)
@@ -473,6 +478,18 @@
         bands[5, y] = own - pltpu.roll(around, 3 * nx3 - 1, 0)[nx3:2 * nx3]
 
     wait_faces(3, q0, ysrcq, ydstq, 2)
+    for side in range(2):
+        there, device = sides[2 + side]
+        copy = pltpu.make_async_remote_copy(
+            src_ref=ysrcw.at[side], dst_ref=ydstw.at[side],
+            send_sem=face_send.at[3, 2 + side], recv_sem=face_recv.at[3, 2 + side],
+            device_id=device, device_id_type=MESH,
+        )
+        pl.when(there)(copy.wait_recv)
+    for side in range(2):
+        wide = split_dot(jnp.concatenate([ydstw[side, j] for j in range(nx1)], axis=0), up0[...])
+        for j in range(nx1):
+            wide_rows[side, j] = wide[j:j + 1]
 
     fold = ny // ny3
 
@@ -491,7 +508,10 @@
             edge = flat + jnp.where(sub == 0, down, 0.0) + jnp.where(sub == fold - 1, up, 0.0)
             for k in range(chunk):
                 i = c * chunk + k
-                centre, near_sum = band_neighbours(q0.at[i + 1], r, ydstq[0, i], ydstq[1, i])
+                centre, near_sum = band_neighbours(
+                    q0.at[i + 1], r,
+                    ydstq[0, i] + wide_rows[0, i // 2] if r == 0 else None,
+                    ydstq[1, i] + wide_rows[1, i // 2] if r == ny // 8 - 1 else None)
                 near_sum += q0[i, band(r), :] + q0[i + 2, band(r), :]
                 precond = centre + own
                 image = 6.0 * centre - near_sum + dg[i, band(r), :] * precond + edge
@@ -535,7 +555,7 @@
     both = jnp.sum(total, axis=1, keepdims=True)
     alpha_ref[...] = jnp.broadcast_to(both[:1] / both[1:], alpha_ref.shape)
 
-    for copies in (copies0, copies1, copies2, copiesq):
+    for copies in (copies0, copies1, copies2, copiesq, copiesw):
         for there, copy in copies:
             pl.when(there)(copy.wait_send)
 
@@ -605,6 +625,7 @@
     scratch = [
         block, block, V(nx + 2, ny, nz), V(nx + 2, ny, nz),
         V(2, nx, 1, nz), V(2, nx, 1, nz), V(2, nx, 1, nz), V(2, nx, 1, nz),
+        V(2, nx1, 1, nz1), V(2, nx1, 1, nz1), V(2, nx1, 1, nz),
         V(2, nz1 // 128, nx1, ny, 128), V(nx1, ny1, nz1), V(nx1 + 2, ny1, nz1),
         V(2, nx1, 1, nz1), V(2, nx1, 1, nz1), V(nz1 // 128, nx1, ny, 128),
         V(2, nx2, ny1, nz2), V(nx2, ny2, nz2), V(nx2 + 2, ny2, nz2),

time: 39.8 us -> 41.2 us (1.035)
  Pallas kernels: 39 us -> 40.4 us
    pallas_call x1, Pallas kernels: 35.5 us -> 36.9 us  [body(): pl.pallas_call(functools.partial(kernel, n_gx, n_gy, nx, ny, nz), out_sha...]
where the time goes in v2:
time: 41.2 us; the launch traced here: 41 us
  Pallas kernels  40.4 us (98%)
  between operations  0.64 us (2%)
    pallas_call x1, Pallas kernels, body(): pl.pallas_call(functools.partial(kernel, n_gx, n_gy, nx, ny, nz), out_sha...  36.9 us
    pallas_call x1, Pallas kernels, body(): pl.pallas_call(functools.partial(scale_kernel, nx), out_shape=(whole, who...  3.48 us

profile of v2, /device:TPU:0, one launch (start us, length us, event | category | flops | bytes accessed | tf_op | source)
XLA Modules:
  0.0 41.0 jit_solution(18339113027940023543)
XLA Ops:
  0.6 36.9 %cycle.1 = (f32[64,32,512]{2,1,0:T(8,128)S(1)}, f32[64,32,512]{2,1,0:T(8,128)S(1)}, f32[64,32,512]{2,1,0:T(8,128)S(1)}, f32[8,128]{1,0:T(8,128)S(1)}) custom-call(f32[64,32,512]{2,1,0:T(8,128)} %rs_hbm.1, f32[64,32,512]{2,1,0:T(8,128)} %dg_hbm.1), custom_call_target="tpu_custom_call" | custom-call | tf_op jit(solution)/shard_map/cycle/pallas_call | solution.py:641
  37.5 3.5 %scale.1 = (f32[64,32,512]{2,1,0:T(8,128)}, f32[64,32,512]{2,1,0:T(8,128)}) custom-call(f32[64,32,512]{2,1,0:T(8,128)S(1)} %get-tuple-element.6.precond, f32[64,32,512]{2,1,0:T(8,128)S(1)} %get-tuple-element.7.image, f32[64,32,512]{2,1,0:T(8,128)S(1)} %get-tuple-element.8.right, f32[8,128]{1,0:T(8,128)S(1)} %get-tuple-element.9.alpha_ref), custom_call_target="tpu_custom_call" | custom-call | tf_op jit(solution)/shard_map/scale/pallas_call | solution.py:652
